TPU v7x, 32 devices: a whole 2x2x4 slice. The times are simulated.
32 devices in a mesh: expert: 8 (over y, x, core), tensor: 4 (over z).
Axes of the slice: x: 2, y: 2, z: 4, core: 2. Of those that a mesh axis runs over, the one named last changes fastest.
Arguments:
- tokens: bfloat16 [1024, 6144], P('expert', 'tensor'), may hold values from -6 to 6
- expert_ids: int32 [1024, 2], P('expert'), may hold values from 0 to 7, all different within a row; in each aligned block of 128 rows (0 to 127, 128 to 255, ...) at most 48 rows name the same one
- gate_fixed: int32 [1024, 2], P('expert'), may hold values from 4096 to 65535
- w_gate: bfloat16 [8, 4096, 6144], P('expert', None, 'tensor'), may hold values from -0.078125 to 0.078125
- w_up: bfloat16 [8, 4096, 6144], P('expert', None, 'tensor'), may hold values from -0.078125 to 0.078125
- w_down: bfloat16 [8, 4096, 6144], P('expert', None, 'tensor'), may hold values from -0.0625 to 0.0625
Outputs:
- mixed: bfloat16 [1024, 6144], P('expert', 'tensor')
Inputs may be any that keep to these rules, and one draw needn't show every extreme that they name: `expert_ids`: each row names 2 different experts. Among the 128 rows of one sequence shard (aligned blocks), no expert is named by more than 48 rows, a bound that some block reaches.
All inputs are finite; a program needn't handle non-finite values.
Results may differ from a plain program's by a relative error of at most 0.0064.
Values may be sent and summed in bfloat16 or wider, within the bound.
A program may use at most 128 MiB of HBM per device.

v0:
```python
import jax
import jax.numpy as jnp
from jax import lax
from jax.sharding import PartitionSpec as P

EXPERTS = 4
CAP = 48


def on_device(tokens, expert_ids, gate_fixed, w_gate, w_up, w_down):
    width_part = tokens.shape[1]
    quarters = lax.axis_size("expert") // EXPERTS
    groups = lax.axis_size("tensor")
    expert_iota = jnp.arange(EXPERTS, dtype=jnp.int32)
    matched = expert_ids[:, :, None] == expert_iota
    routed = jnp.sum(matched.astype(jnp.int32), axis=1)
    weights = (
        jnp.sum(jnp.where(matched, gate_fixed[:, :, None], 0), axis=1).astype(jnp.float32) / 65536.0
    )
    position = jnp.cumsum(routed, axis=0) - routed
    slot_iota = jnp.arange(CAP, dtype=jnp.int32)
    placed = (position[:, :, None] == slot_iota) & (routed[:, :, None] > 0)
    outgoing = jnp.einsum(
        "tec,td->ecd", placed.astype(jnp.bfloat16), tokens, preferred_element_type=jnp.float32
    ).astype(jnp.bfloat16)
    outgoing = jnp.tile(outgoing, (quarters, 1, 1))
    arrived = lax.all_to_all(outgoing, "expert", split_axis=0, concat_axis=0, tiled=True)
    sources = arrived.shape[0]
    total_rows = sources * CAP
    rows_in = arrived.reshape(total_rows, width_part)
    gate_local = w_gate[0]
    up_local = w_up[0]
    down_local = w_down[0]
    hidden_width = gate_local.shape[0]
    contract = (((1,), (1,)), ((), ()))
    gate_term = lax.dot_general(
        rows_in, gate_local, contract, preferred_element_type=jnp.float32
    ).astype(jnp.bfloat16)
    up_term = lax.dot_general(
        rows_in, up_local, contract, preferred_element_type=jnp.float32
    ).astype(jnp.bfloat16)
    gate_parts, up_parts = (
        lax.all_to_all(gate_term, "tensor", split_axis=0, concat_axis=0, tiled=True),
        lax.all_to_all(up_term, "tensor", split_axis=0, concat_axis=0, tiled=True),
    )
    row_share = total_rows // groups
    gate_share = jnp.sum(
        gate_parts.reshape(groups, row_share, hidden_width).astype(jnp.float32), axis=0
    )
    up_share = jnp.sum(
        up_parts.reshape(groups, row_share, hidden_width).astype(jnp.float32), axis=0
    )
    hidden = (jax.nn.silu(gate_share) * up_share).astype(jnp.bfloat16)
    partial_out = jnp.dot(
        lax.all_gather(hidden, "tensor", axis=0, tiled=True),
        down_local,
        preferred_element_type=jnp.float32,
    )
    returned = lax.all_to_all(
        partial_out.reshape(sources, CAP, width_part),
        "expert",
        split_axis=0,
        concat_axis=0,
        tiled=True,
    )
    summed = jnp.sum(returned.reshape(quarters, EXPERTS, CAP, width_part), axis=0)
    selector = placed.astype(jnp.float32) * weights[:, :, None]
    mixed = jnp.einsum("tec,ecd->td", selector, summed, precision=lax.Precision.HIGHEST)
    return mixed.astype(jnp.bfloat16)


def solution(mesh):
    placed = (
        P("expert", "tensor"),
        P("expert", None),
        P("expert", None),
        P("expert", None, "tensor"),
        P("expert", None, "tensor"),
        P("expert", None, "tensor"),
    )
    return jax.shard_map(
        on_device, mesh=mesh, in_specs=placed, out_specs=P("expert", "tensor"), check_vma=False
    )
```

profile of v0, /device:TPU:1, one launch (start us, length us, event | category | flops | bytes accessed | tf_op | source)
XLA Modules:
  0.0 315.5 jit_solution(17452105364876924416)
XLA Ops:
  6.5 0.0 copy-start
  6.5 0.8 select_reduce_fusion
  7.3 0.1 copy.11
  7.4 0.2 reduce_window_sum.11
  7.6 0.1 copy.13
  7.7 0.0 copy-done
  7.7 0.3 convolution_convert_fusion
  8.0 0.1 tile.4
  8.1 20.9 %all_to_all.28 = bf16[8,48,1536]{2,1,0:T(8,128)(2,1)S(1)} all-to-all(bf16[8,48,1536]{2,1,0:T(8,128)(2,1)S(1)} %bitcast.32), channel_id=1, replica_groups=mesh['expert'=8,'tensor'=4] {'expert'}, dimensions={0} | all-to-all | bytes 2359296 | tf_op jit(solution)/shard_map/all_to_all | solution.py:27
  29.0 0.0 copy-start.3
  29.0 18.4 %fusion.9 = bf16[384,4096]{1,0:T(8,128)(2,1)} fusion(bf16[384,1536]{1,0:T(8,128)(2,1)S(1)} %bitcast.35, bf16[1,4096,1536]{2,1,0:T(8,128)(2,1)} %param.10), kind=kOutput, calls=%fused_computation.9 | convolution fusion | flops 4833411072 | bytes 16908288 | tf_op jit(solution)/shard_map/dot_general | solution.py:39
  47.4 0.0 copy-done.3
  47.4 4.6 %all-to-all-start.2 = ((bf16[4,96,4096]{2,1,0:T(8,128)(2,1)}), bf16[4,96,4096]{2,1,0:T(8,128)(2,1)S(1)}, u32[]{:S(2)}, u32[]{:S(2)}) async-start(bf16[4,96,4096]{2,1,0:T(8,128)(2,1)} %bitcast.34), calls=%async_computation.2 | async-start | bytes 6291456 | tf_op jit(solution)/shard_map/all_to_all | solution.py:44
  52.0 9.5 %fusion.6 = bf16[384,4096]{1,0:T(8,128)(2,1)} fusion(bf16[384,1536]{1,0:T(8,128)(2,1)} %bitcast.36, bf16[1,4096,1536]{2,1,0:T(8,128)(2,1)} %param.9), kind=kOutput, calls=%fused_computation.8 | convolution fusion | flops 4833411072 | bytes 16908288 | tf_op jit(solution)/shard_map/dot_general | solution.py:36
  61.6 60.6 %all-to-all-done.2 = bf16[4,96,4096]{2,1,0:T(8,128)(2,1)S(1)} async-done(((bf16[4,96,4096]{2,1,0:T(8,128)(2,1)}), bf16[4,96,4096]{2,1,0:T(8,128)(2,1)S(1)}, u32[]{:S(2)}, u32[]{:S(2)}) %all-to-all-start.2) | async-done | bytes 3145760 | tf_op jit(solution)/shard_map/all_to_all | solution.py:44
  122.2 4.6 %all-to-all-start.1 = ((bf16[4,96,4096]{2,1,0:T(8,128)(2,1)}), bf16[4,96,4096]{2,1,0:T(8,128)(2,1)}, u32[]{:S(2)}, u32[]{:S(2)}) async-start(bf16[4,96,4096]{2,1,0:T(8,128)(2,1)} %bitcast.33), calls=%async_computation.1 | async-start | bytes 6291456 | tf_op jit(solution)/shard_map/all_to_all | solution.py:43
  126.8 0.0 all-gather.2.cloned.1.call-start
  126.9 1.7 convert_reduce_fusion
  128.5 0.0 copy-start.2
  128.6 68.5 %all-to-all-done.1 = bf16[4,96,4096]{2,1,0:T(8,128)(2,1)} async-done(((bf16[4,96,4096]{2,1,0:T(8,128)(2,1)}), bf16[4,96,4096]{2,1,0:T(8,128)(2,1)}, u32[]{:S(2)}, u32[]{:S(2)}) %all-to-all-start.1) | async-done | bytes 3145760 | tf_op jit(solution)/shard_map/all_to_all | solution.py:43
  197.1 2.6 convert_reduce_fusion.1
  199.7 0.0 copy-done.2
  199.7 1.3 multiply_convert_fusion
  201.0 0.0 all-gather.2.cloned.1.call-update
  201.0 61.8 %all-gather.2.cloned.1.call-done = bf16[384,4096]{1,0:T(8,128)(2,1)} async-done(((bf16[96,4096]{1,0:T(8,128)(2,1)}), bf16[384,4096]{1,0:T(8,128)(2,1)}) %all-gather.2.cloned.1.call-update) | async-done | bytes 3145744 | tf_op jit(solution)/shard_map/all_gather | solution.py:55
  262.8 11.3 %fusion = f32[8,48,1536]{2,1,0:T(8,128)} fusion(bf16[8,48,4096]{2,1,0:T(8,128)(2,1)} %bitcast.37, bf16[1,4096,1536]{2,1,0:T(8,128)(2,1)} %param.11), kind=kOutput, calls=%fused_computation | convolution fusion | flops 4831838208 | bytes 18087936 | tf_op jit(solution)/shard_map/dot_general | solution.py:54
  274.1 4.4 %all-to-all-start.3 = ((f32[8,48,1536]{2,1,0:T(8,128)}), f32[8,48,1536]{2,1,0:T(8,128)S(1)}, u32[]{:S(2)}, u32[]{:S(2)}) async-start(f32[8,48,1536]{2,1,0:T(8,128)} %fusion), calls=%async_computation.3 | async-start | bytes 4718592 | tf_op jit(solution)/shard_map/all_to_all | solution.py:59
  278.5 26.0 %all-to-all-done.3 = f32[8,48,1536]{2,1,0:T(8,128)S(1)} async-done(((f32[8,48,1536]{2,1,0:T(8,128)}), f32[8,48,1536]{2,1,0:T(8,128)S(1)}, u32[]{:S(2)}, u32[]{:S(2)}) %all-to-all-start.3) | async-done | bytes 2359328 | tf_op jit(solution)/shard_map/all_to_all | solution.py:59
  304.5 0.0 copy-start.1
  304.5 1.3 reduce_sum.49
  305.8 2.9 fusion.12
  308.7 0.0 copy-done.1
  (3 shorter events, 0.0 us)
Async XLA Ops:
  6.5 1.1 copy-start
  29.0 18.4 %copy-start.3 = (bf16[8,48,1536]{2,1,0:T(8,128)(2,1)}, bf16[8,48,1536]{2,1,0:T(8,128)(2,1)S(1)}, u32[]{:S(2)}) copy-start(bf16[8,48,1536]{2,1,0:T(8,128)(2,1)S(1)} %all_to_all.28) | copy-start | bytes 3538948
  47.4 74.7 %all-to-all-start.2 = ((bf16[4,96,4096]{2,1,0:T(8,128)(2,1)}), bf16[4,96,4096]{2,1,0:T(8,128)(2,1)S(1)}, u32[]{:S(2)}, u32[]{:S(2)}) async-start(bf16[4,96,4096]{2,1,0:T(8,128)(2,1)} %bitcast.34), calls=%async_computation.2 | async-start | bytes 6291456 | tf_op jit(solution)/shard_map/all_to_all | solution.py:44
  122.2 74.9 %all-to-all-start.1 = ((bf16[4,96,4096]{2,1,0:T(8,128)(2,1)}), bf16[4,96,4096]{2,1,0:T(8,128)(2,1)}, u32[]{:S(2)}, u32[]{:S(2)}) async-start(bf16[4,96,4096]{2,1,0:T(8,128)(2,1)} %bitcast.33), calls=%async_computation.1 | async-start | bytes 6291456 | tf_op jit(solution)/shard_map/all_to_all | solution.py:43
  126.8 136.0 %all-gather.2.cloned.1.call-start = ((), (), s32[]{:S(2)}) async-start(), calls=%async_computation.4 | async-start | bytes 3932160 | tf_op jit(solution)/shard_map/all_gather | solution.py:55
  128.5 71.1 %copy-start.2 = (f32[96,4096]{1,0:T(8,128)S(1)}, f32[96,4096]{1,0:T(8,128)}, u32[]{:S(2)}) copy-start(f32[96,4096]{1,0:T(8,128)} %convert_reduce_fusion) | copy-start | bytes 4718596
  274.1 30.4 %all-to-all-start.3 = ((f32[8,48,1536]{2,1,0:T(8,128)}), f32[8,48,1536]{2,1,0:T(8,128)S(1)}, u32[]{:S(2)}, u32[]{:S(2)}) async-start(f32[8,48,1536]{2,1,0:T(8,128)} %fusion), calls=%async_computation.3 | async-start | bytes 4718592 | tf_op jit(solution)/shard_map/all_to_all | solution.py:59
  304.5 4.2 %copy-start.1 = (bf16[128,1536]{1,0:T(8,128)(2,1)S(1)}, bf16[128,1536]{1,0:T(8,128)(2,1)}, u32[]{:S(2)}) copy-start(bf16[128,1536]{1,0:T(8,128)(2,1)} %param.6) | copy-start | bytes 1179652
Sparse Core Ops, SparseCore 0:
  201.1 61.6 all-gather.1
where the time goes:
time: 319 us; the launch traced here: 316 us
  waiting for transfers between devices  217 us (68%)
  matrix products  42.5 us (13%)
  blocking collectives  20.9 us (7%)
  starting transfers between devices  13.6 us (4%)
  between operations  13.4 us (4%)
  other arithmetic  7.81 us (2%)
    all_to_all x1, waiting for transfers between devices, on_device(): lax.all_to_all(gate_term, 'tensor', split_axis=0, concat_axis=0, tiled=True)  68.5 us
    all_gather x1, waiting for transfers between devices, on_device(): lax.all_gather(hidden, 'tensor', axis=0, tiled=True)  61.8 us
    all_to_all x1, waiting for transfers between devices, on_device(): lax.all_to_all(up_term, 'tensor', split_axis=0, concat_axis=0, tiled=True)  60.6 us
    all_to_all x1, waiting for transfers between devices, on_device(): lax.all_to_all(partial_out.reshape(sources, CAP, width_part), 'expert', s...  26 us
    all_to_all x1, blocking collectives, on_device(): lax.all_to_all(outgoing, 'expert', split_axis=0, concat_axis=0, tiled=True)  20.9 us
    dot_general x1, matrix products, on_device(): lax.dot_general(rows_in, up_local, contract, preferred_element_type=jnp.f...  18.4 us
    dot_general x1, matrix products, on_device(): jnp.dot(lax.all_gather(hidden, 'tensor', axis=0, tiled=True), down_local,...  11.3 us
    dot_general x1, matrix products, on_device(): lax.dot_general(rows_in, gate_local, contract, preferred_element_type=jnp...  9.53 us
  transfers between devices with their start and end apart: 4, of which 4 were waited for; matrix products, arithmetic and copies ran while one was open for 4% of the time, Pallas kernels for 0%

commit v1 on v0

v1 whole, which is shorter than its diff:
```python
import functools

import jax
import jax.numpy as jnp
from jax import lax
from jax.experimental import pallas as pl
from jax.experimental.pallas import tpu as pltpu
from jax.sharding import PartitionSpec as P

EXPERTS = 4
CAP = 48
MESH = pl.DeviceIdType.MESH
CHUNK = 256
SKEW = 2
LINE = 4
CONTRACT_LAST = (((1,), (1,)), ((), ()))


def line_kernel(
    devices, groups, cap, chunk,
    outgoing, high, low, w_gate, w_up, w_down, mixed,
    gate_v, up_v, down_v, rows, running, term, hidden, total, returned,
    gate_sem, up_sem, down_sem, out_send, out_recv, back_send, back_recv,
    run_send, run_recv, hid_send, hid_recv,
):
    me, at = lax.axis_index("expert"), lax.axis_index("tensor")
    held = outgoing.shape[0]
    half = devices * cap // 2
    count = w_gate.shape[1] // chunk
    last = groups - 1
    place = (last - at, at)
    onward = (at - 1, at + 1)
    before = (at + 1, at - 1)
    ahead = jnp.minimum(place[0], place[1])
    behind = jnp.maximum(place[0], place[1])

    def weight(source, target, sem, c):
        cut = pl.ds(pl.multiple_of(c * chunk, chunk), chunk)
        return pltpu.make_async_copy(source.at[0, cut, :], target.at[cut, :], sem.at[c])

    def start_first(c, carry):
        weight(w_gate, gate_v, gate_sem, c).start()
        weight(w_up, up_v, up_sem, c).start()
        return carry

    def start_second(c, carry):
        weight(w_down, down_v, down_sem, c).start()
        return carry

    lax.fori_loop(0, count, start_first, 0)

    barrier = pltpu.get_barrier_semaphore()
    for k in range(1, devices):
        peer = lax.rem(me + k, devices)
        pl.semaphore_signal(barrier, inc=1, device_id={"expert": peer}, device_id_type=MESH)

    @pl.when(at > 0)
    def _():
        pl.semaphore_signal(barrier, inc=1, device_id={"tensor": at - 1}, device_id_type=MESH)

    @pl.when(at < last)
    def _():
        pl.semaphore_signal(barrier, inc=1, device_id={"tensor": at + 1}, device_id_type=MESH)

    inside = (at > 0) & (at < last)

    @pl.when(inside)
    def _():
        pl.semaphore_wait(barrier, devices + 1)

    @pl.when(jnp.logical_not(inside))
    def _():
        pl.semaphore_wait(barrier, devices - 1 + min(last, 1))

    def block(shard):
        return pl.ds(pl.multiple_of(shard * cap, cap), cap)

    def dispatch(peer):
        return pltpu.make_async_remote_copy(
            src_ref=outgoing.at[lax.rem(peer, held)],
            dst_ref=rows.at[block(me), :],
            send_sem=out_send.at[peer],
            recv_sem=out_recv.at[me],
            device_id={"expert": peer},
            device_id_type=MESH,
        )

    def arrived(peer):
        return pltpu.make_async_remote_copy(
            src_ref=outgoing.at[0],
            dst_ref=rows.at[block(peer), :],
            send_sem=out_send.at[peer],
            recv_sem=out_recv.at[peer],
            device_id={"expert": peer},
            device_id_type=MESH,
        )

    for k in range(1, devices):
        dispatch(lax.rem(me + k, devices)).start()
    lax.fori_loop(0, count, start_second, 0)
    rows[block(me), :] = outgoing[lax.rem(me, held)]
    total[...] = jnp.zeros_like(total)
    for k in range(1, devices):
        arrived(lax.rem(me + devices - k, devices)).wait_recv()

    def run_copy(s, c):
        return pltpu.make_async_remote_copy(
            src_ref=running.at[s, c],
            dst_ref=running.at[s, c],
            send_sem=run_send.at[s, c],
            recv_sem=run_recv.at[s, c],
            device_id={"tensor": onward[s]},
            device_id_type=MESH,
        )

    def hid_copy(s, c):
        return pltpu.make_async_remote_copy(
            src_ref=hidden.at[s, c],
            dst_ref=hidden.at[s, c],
            send_sem=hid_send.at[s, c],
            recv_sem=hid_recv.at[s, c],
            device_id={"tensor": before[s]},
            device_id_type=MESH,
        )

    def step(t, carry):
        fresh = t - SKEW * ahead

        @pl.when((fresh >= 0) & (fresh < count))
        def _():
            weight(w_gate, gate_v, gate_sem, fresh).wait()
            weight(w_up, up_v, up_sem, fresh).wait()

        for s in (0, 1):
            c = t - SKEW * place[s]

            @pl.when((c >= 0) & (c < count))
            def _(s=s, c=c):
                cut = pl.ds(pl.multiple_of(c * chunk, chunk), chunk)
                own = rows[s * half : (s + 1) * half, :]
                term[:, :chunk] = lax.dot_general(
                    own, gate_v[cut, :], CONTRACT_LAST, preferred_element_type=jnp.float32
                )
                term[:, chunk:] = lax.dot_general(
                    own, up_v[cut, :], CONTRACT_LAST, preferred_element_type=jnp.float32
                )

                @pl.when(place[s] == 0)
                def _():
                    running[s, c] = term[...].astype(jnp.bfloat16)
                    run_copy(s, c).start()

                @pl.when((place[s] > 0) & (place[s] < last))
                def _():
                    run_copy(s, c).wait_recv()
                    running[s, c] = (running[s, c].astype(jnp.float32) + term[...]).astype(
                        jnp.bfloat16
                    )
                    run_copy(s, c).start()

                @pl.when(place[s] == last)
                def _():
                    run_copy(s, c).wait_recv()
                    whole = running[s, c].astype(jnp.float32) + term[...]
                    gate, up = whole[:, :chunk], whole[:, chunk:]
                    hidden[s, c] = (gate / (1.0 + jnp.exp(-gate)) * up).astype(jnp.bfloat16)
                    hid_copy(s, c).start()

        for s in (0, 1):
            c = t - 2 * SKEW * last + SKEW * place[s]

            @pl.when((c >= 0) & (c < count) & (place[s] < last))
            def _(s=s, c=c):
                hid_copy(s, c).wait_recv()

                @pl.when(place[s] > 0)
                def _():
                    hid_copy(s, c).start()

        ripe = t - 2 * SKEW * last + SKEW * behind

        @pl.when((ripe >= 0) & (ripe < count))
        def _():
            weight(w_down, down_v, down_sem, ripe).wait()

        for s in (0, 1):
            c = t - 2 * SKEW * last + SKEW * place[s]

            @pl.when((c >= 0) & (c < count))
            def _(s=s, c=c):
                cut = pl.ds(pl.multiple_of(c * chunk, chunk), chunk)
                total[s] += jnp.dot(
                    hidden[s, c], down_v[cut, :], preferred_element_type=jnp.float32
                )

        return carry

    lax.fori_loop(0, count + 2 * SKEW * last, step, 0)

    rows[:half, :] = total[0].astype(jnp.bfloat16)
    rows[half:, :] = total[1].astype(jnp.bfloat16)

    def back(peer):
        return pltpu.make_async_remote_copy(
            src_ref=rows.at[block(peer), :],
            dst_ref=returned.at[block(me), :],
            send_sem=back_send.at[peer],
            recv_sem=back_recv.at[me],
            device_id={"expert": peer},
            device_id_type=MESH,
        )

    def came_back(peer):
        return pltpu.make_async_remote_copy(
            src_ref=rows.at[block(peer), :],
            dst_ref=returned.at[block(peer), :],
            send_sem=back_send.at[peer],
            recv_sem=back_recv.at[peer],
            device_id={"expert": peer},
            device_id_type=MESH,
        )

    for k in range(1, devices):
        back(lax.rem(me + k, devices)).start()
    returned[block(me), :] = rows[block(me), :]

    def drain(c, carry):
        for s in (0, 1):

            @pl.when(place[s] < last)
            def _(s=s):
                run_copy(s, c).wait_send()

            @pl.when(place[s] > 0)
            def _(s=s):
                hid_copy(s, c).wait_send()

        return carry

    lax.fori_loop(0, count, drain, 0)
    for k in range(1, devices):
        dispatch(lax.rem(me + k, devices)).wait_send()
    for k in range(1, devices):
        came_back(lax.rem(me + devices - k, devices)).wait_recv()
    coarse = jnp.dot(high[...], returned[...], preferred_element_type=jnp.float32)
    fine = jnp.dot(low[...], returned[...], preferred_element_type=jnp.float32)
    mixed[...] = ((coarse * 256.0 + fine) * (1.0 / 65536.0)).astype(mixed.dtype)
    for k in range(1, devices):
        back(lax.rem(me + k, devices)).wait_send()


def along_line(outgoing, high, low, w_gate, w_up, w_down, devices, groups, cap):
    token_count, width_part = high.shape[0], outgoing.shape[2]
    hidden_width = w_gate.shape[1]
    chunk = min(CHUNK, hidden_width)
    count = hidden_width // chunk
    half = devices * cap // 2
    in_vmem, in_place = pl.BlockSpec(memory_space=pltpu.VMEM), pl.BlockSpec(memory_space=pl.ANY)
    flops = 2 * 3 * 2 * half * hidden_width * width_part
    return pl.pallas_call(
        functools.partial(line_kernel, devices, groups, cap, chunk),
        out_shape=jax.ShapeDtypeStruct((token_count, width_part), jnp.bfloat16),
        in_specs=[in_vmem] * 3 + [in_place] * 3,
        out_specs=in_vmem,
        scratch_shapes=[
            pltpu.VMEM((hidden_width, width_part), jnp.bfloat16),
            pltpu.VMEM((hidden_width, width_part), jnp.bfloat16),
            pltpu.VMEM((hidden_width, width_part), jnp.bfloat16),
            pltpu.VMEM((2 * half, width_part), jnp.bfloat16),
            pltpu.VMEM((2, count, half, 2 * chunk), jnp.bfloat16),
            pltpu.VMEM((half, 2 * chunk), jnp.float32),
            pltpu.VMEM((2, count, half, chunk), jnp.bfloat16),
            pltpu.VMEM((2, half, width_part), jnp.float32),
            pltpu.VMEM((2 * half, width_part), jnp.bfloat16),
            *[pltpu.SemaphoreType.DMA((count,))] * 3,
            *[pltpu.SemaphoreType.DMA((devices,))] * 4,
            *[pltpu.SemaphoreType.DMA((2, count))] * 4,
        ],
        compiler_params=pltpu.CompilerParams(
            collective_id=0, has_side_effects=True, vmem_limit_bytes=60 * 2**20
        ),
        cost_estimate=pl.CostEstimate(
            flops=flops,
            bytes_accessed=3 * 2 * hidden_width * width_part,
            transcendentals=half * hidden_width,
        ),
    )(outgoing, high, low, w_gate, w_up, w_down)


def by_collectives(outgoing, high, low, w_gate, w_up, w_down, devices, groups, cap):
    width_part = outgoing.shape[2]
    arrived = lax.all_to_all(
        jnp.tile(outgoing, (devices // EXPERTS, 1, 1)), "expert", split_axis=0, concat_axis=0, tiled=True
    )
    total_rows = devices * cap
    rows_in = arrived.reshape(total_rows, width_part)
    hidden_width = w_gate.shape[1]

    def summed(weights):
        product = lax.dot_general(
            rows_in, weights[0], CONTRACT_LAST, preferred_element_type=jnp.float32
        ).astype(jnp.bfloat16)
        parts = lax.all_to_all(product, "tensor", split_axis=0, concat_axis=0, tiled=True)
        parts = parts.reshape(groups, total_rows // groups, hidden_width)
        return jnp.sum(parts.astype(jnp.float32), axis=0)

    hidden = (jax.nn.silu(summed(w_gate)) * summed(w_up)).astype(jnp.bfloat16)
    partial_out = jnp.dot(
        lax.all_gather(hidden, "tensor", axis=0, tiled=True),
        w_down[0],
        preferred_element_type=jnp.float32,
    )
    returned = lax.all_to_all(
        partial_out.reshape(devices, cap, width_part), "expert", split_axis=0, concat_axis=0, tiled=True
    )
    selector = (high.astype(jnp.float32) * 256.0 + low.astype(jnp.float32)) / 65536.0
    mixed = jnp.dot(
        selector, returned.reshape(total_rows, width_part), precision=lax.Precision.HIGHEST
    )
    return mixed.astype(jnp.bfloat16)


def on_device(tokens, expert_ids, gate_fixed, w_gate, w_up, w_down, cap=CAP):
    devices = lax.axis_size("expert")
    groups = lax.axis_size("tensor")
    token_count = tokens.shape[0]
    matched = expert_ids[:, :, None] == jnp.arange(EXPERTS, dtype=jnp.int32)
    routed = jnp.any(matched, axis=1)
    units = jnp.sum(jnp.where(matched, gate_fixed[:, :, None], 0), axis=1)
    order = jnp.arange(token_count, dtype=jnp.int32)
    earlier = (order[:, None] > order[None, :]).astype(jnp.bfloat16)
    position = jnp.dot(
        earlier, routed.astype(jnp.bfloat16), preferred_element_type=jnp.float32
    ).astype(jnp.int32)
    slots = jnp.arange(cap, dtype=jnp.int32)
    placed = (position[:, :, None] == slots) & routed[:, :, None]
    outgoing = jnp.einsum(
        "tec,td->ecd", placed.astype(jnp.bfloat16), tokens, preferred_element_type=jnp.float32
    ).astype(jnp.bfloat16)

    def selector(digit):
        chosen = jnp.where(placed, digit[:, :, None], 0).astype(jnp.bfloat16)
        return jnp.tile(chosen.reshape(token_count, EXPERTS * cap), (1, devices // EXPERTS))

    high, low = selector(units // 256), selector(units % 256)
    plan = along_line if groups <= LINE else by_collectives
    return plan(outgoing, high, low, w_gate, w_up, w_down, devices, groups, cap)


def solution(mesh):
    placed = (
        P("expert", "tensor"),
        P("expert", None),
        P("expert", None),
        P("expert", None, "tensor"),
        P("expert", None, "tensor"),
        P("expert", None, "tensor"),
    )
    return jax.shard_map(
        on_device, mesh=mesh, in_specs=placed, out_specs=P("expert", "tensor"), check_vma=False
    )
```

time: 319 us -> 161 us (0.50)
  waiting for transfers between devices: 217 us -> 0 us
  Pallas kernels: 0 us -> 154 us
  matrix products: 42.5 us -> 1.26 us
  blocking collectives: 20.9 us -> 0 us
  starting transfers between devices: 13.6 us -> 0 us
  between operations: 13.4 us -> 0.04 us
  other arithmetic: 7.81 us -> 1.58 us
    all_to_all x3 -> x0, waiting for transfers between devices: 155 us -> none  [the longest x1 68.5 us: on_device(): lax.all_to_all(gate_term, 'tensor', split_axis=0, concat_axis=0, tiled=True)]
    pallas_call x0 -> x1, Pallas kernels: none -> 154 us  [along_line(): pl.pallas_call(functools.partial(line_kernel, devices, groups, cap, chunk...]
    all_gather x1 -> x0, waiting for transfers between devices: 61.8 us -> none  [on_device(): lax.all_gather(hidden, 'tensor', axis=0, tiled=True)]
    dot_general x4 -> x1, matrix products: 42.2 us -> 0.14 us  [on_device(): jnp.dot(earlier, routed.astype(jnp.bfloat16), preferred_element_type=jnp....]
    all_to_all x1 -> x0, blocking collectives: 20.9 us -> none  [on_device(): lax.all_to_all(outgoing, 'expert', split_axis=0, concat_axis=0, tiled=True)]
    all_to_all x3 -> x0, starting transfers between devices: 13.6 us -> none  [the longest x1 4.64 us: on_device(): lax.all_to_all(gate_term, 'tensor', split_axis=0, concat_axis=0, tiled=True)]
    reduce_sum x4 -> x1, other arithmetic: 6.31 us -> 0.73 us  [on_device(): units = jnp.sum(jnp.where(matched, gate_fixed[:, :, None], 0), axis=1)]
  transfers between devices with their start and end apart: 4 -> 0, of which waited for: 4 -> 0; matrix products, arithmetic and copies ran while one was open for 4% -> 0% of each run, Pallas kernels for 0% -> 0%
where the time goes in v1:
time: 161 us
  Pallas kernels  154 us (96%)
  local copies, waits for them, and re-layouts  3.38 us (2%)
    pallas_call x1, Pallas kernels, along_line(): pl.pallas_call(functools.partial(line_kernel, devices, groups, cap, chunk...  154 us

profile of v1, /device:TPU:1, one launch (start us, length us, event | category | flops | bytes accessed | tf_op | source)
XLA Modules:
  0.0 160.7 jit_solution(10572856707177074893)
XLA Ops:
  0.0 0.0 copy-start
  0.0 0.7 fusion.8
  0.7 0.1 convolution_convert_fusion.1
  0.9 0.7 select_reduce_fusion
  1.6 0.1 eq.53
  1.7 0.1 fusion.1
  1.8 0.7 copy.16.low
  2.6 0.8 copy.15.high
  3.3 0.0 copy-done
  3.3 1.1 convolution_convert_fusion.outgoing
  4.5 154.4 %shard_map.64 = bf16[128,1536]{1,0:T(8,128)(2,1)} custom-call(bf16[4,48,1536]{2,1,0:T(8,128)(2,1)} %convolution_convert_fusion.outgoing, bf16[128,384]{1,0:T(8,128)(2,1)} %copy.15.high, bf16[128,384]{1,0:T(8,128)(2,1)} %copy.16.low, bf16[1,4096,1536]{2,1,0:T(8,128)(2,1)} %w_gate.1, bf16[1,4096,1536]{2,1,0:T(8,128)(2,1)} %w_up.1, bf16[1,4096,1536]{2,1,0:T(8,128)(2,1)} %w_down.1), custom_call_target="tpu_custom_call" | custom-call | flops 14495514624 | bytes 37748736 | tf_op jit(solution)/shard_map/pallas_call | solution.py:260
  158.9 1.8 %copy.18 = bf16[128,1536]{1,0:T(8,128)(2,1)} copy(bf16[128,1536]{1,0:T(8,128)(2,1)} %shard_map.64) | data formatting | bytes 786432
  (4 shorter events, 0.0 us)
Async XLA Ops:
  0.0 3.3 %copy-start = (bf16[128,1536]{1,0:T(8,128)(2,1)S(1)}, bf16[128,1536]{1,0:T(8,128)(2,1)}, u32[]{:S(2)}) copy-start(bf16[128,1536]{1,0:T(8,128)(2,1)} %param.6) | copy-start | bytes 1179652

commit v2 on v1

--- a/solution.py
+++ b/solution.py
@@ -13,6 +13,7 @@
 CHUNK = 256
 SKEW = 2
 LINE = 4
+ORDER = {4: (0, 1, 2, 3), 8: (0, 1, 6, 7, 2, 3, 4, 5)}
 CONTRACT_LAST = (((1,), (1,)), ((), ()))
 
 
@@ -25,8 +26,9 @@
 ):
     me, at = lax.axis_index("expert"), lax.axis_index("tensor")
     held = outgoing.shape[0]
-    half = devices * cap // 2
+    part = devices * cap // 4
     count = w_gate.shape[1] // chunk
+    order = ORDER[devices]
     last = groups - 1
     place = (last - at, at)
     onward = (at - 1, at + 1)
@@ -75,33 +77,42 @@
     def block(shard):
         return pl.ds(pl.multiple_of(shard * cap, cap), cap)
 
-    def dispatch(peer):
+    def partner(slot):
+        peer = 0
+        for bit in (1, 2, 4):
+            if bit < devices:
+                peer += lax.rem(lax.div(me, bit) + order[slot] // bit % 2, 2) * bit
+        return peer
+
+    def dispatch(slot):
+        peer = partner(slot)
         return pltpu.make_async_remote_copy(
             src_ref=outgoing.at[lax.rem(peer, held)],
-            dst_ref=rows.at[block(me), :],
-            send_sem=out_send.at[peer],
-            recv_sem=out_recv.at[me],
+            dst_ref=rows.at[slot * cap : (slot + 1) * cap, :],
+            send_sem=out_send.at[slot],
+            recv_sem=out_recv.at[slot],
             device_id={"expert": peer},
             device_id_type=MESH,
         )
 
-    def arrived(peer):
+    def back(slot):
+        peer = partner(slot)
         return pltpu.make_async_remote_copy(
-            src_ref=outgoing.at[0],
-            dst_ref=rows.at[block(peer), :],
-            send_sem=out_send.at[peer],
-            recv_sem=out_recv.at[peer],
+            src_ref=rows.at[slot * cap : (slot + 1) * cap, :],
+            dst_ref=returned.at[block(me), :],
+            send_sem=back_send.at[slot],
+            recv_sem=back_recv.at[slot],
             device_id={"expert": peer},
             device_id_type=MESH,
         )
 
-    for k in range(1, devices):
-        dispatch(lax.rem(me + k, devices)).start()
+    for slot in range(1, devices):
+        dispatch(slot).start()
     lax.fori_loop(0, count, start_second, 0)
-    rows[block(me), :] = outgoing[lax.rem(me, held)]
+    rows[:cap, :] = outgoing[lax.rem(me, held)]
     total[...] = jnp.zeros_like(total)
-    for k in range(1, devices):
-        arrived(lax.rem(me + devices - k, devices)).wait_recv()
+    for slot in range(1, devices // 2):
+        dispatch(slot).wait_recv()
 
     def run_copy(s, c):
         return pltpu.make_async_remote_copy(
@@ -131,13 +142,19 @@
             weight(w_gate, gate_v, gate_sem, fresh).wait()
             weight(w_up, up_v, up_sem, fresh).wait()
 
+        @pl.when(fresh == count)
+        def _():
+            for slot in range(devices // 2, devices):
+                dispatch(slot).wait_recv()
+
         for s in (0, 1):
             c = t - SKEW * place[s]
 
-            @pl.when((c >= 0) & (c < count))
+            @pl.when((c >= 0) & (c < 2 * count))
             def _(s=s, c=c):
-                cut = pl.ds(pl.multiple_of(c * chunk, chunk), chunk)
-                own = rows[s * half : (s + 1) * half, :]
+                cut = pl.ds(pl.multiple_of(lax.rem(c, count) * chunk, chunk), chunk)
+                group = 2 * lax.div(c, count) + s
+                own = rows[pl.ds(pl.multiple_of(group * part, part), part), :]
                 term[:, :chunk] = lax.dot_general(
                     own, gate_v[cut, :], CONTRACT_LAST, preferred_element_type=jnp.float32
                 )
@@ -169,7 +186,7 @@
         for s in (0, 1):
             c = t - 2 * SKEW * last + SKEW * place[s]
 
-            @pl.when((c >= 0) & (c < count) & (place[s] < last))
+            @pl.when((c >= 0) & (c < 2 * count) & (place[s] < last))
             def _(s=s, c=c):
                 hid_copy(s, c).wait_recv()
 
@@ -186,43 +203,26 @@
         for s in (0, 1):
             c = t - 2 * SKEW * last + SKEW * place[s]
 
-            @pl.when((c >= 0) & (c < count))
+            @pl.when((c >= 0) & (c < 2 * count))
             def _(s=s, c=c):
-                cut = pl.ds(pl.multiple_of(c * chunk, chunk), chunk)
-                total[s] += jnp.dot(
+                cut = pl.ds(pl.multiple_of(lax.rem(c, count) * chunk, chunk), chunk)
+                total[2 * lax.div(c, count) + s] += jnp.dot(
                     hidden[s, c], down_v[cut, :], preferred_element_type=jnp.float32
                 )
 
+            for later in (0, 1):
+
+                @pl.when(c == (later + 1) * count - 1)
+                def _(group=2 * later + s):
+                    rows[group * part : (group + 1) * part, :] = total[group].astype(jnp.bfloat16)
+                    for slot in range(group * devices // 4, (group + 1) * devices // 4):
+                        if slot > 0:
+                            back(slot).start()
+
         return carry
 
-    lax.fori_loop(0, count + 2 * SKEW * last, step, 0)
-
-    rows[:half, :] = total[0].astype(jnp.bfloat16)
-    rows[half:, :] = total[1].astype(jnp.bfloat16)
-
-    def back(peer):
-        return pltpu.make_async_remote_copy(
-            src_ref=rows.at[block(peer), :],
-            dst_ref=returned.at[block(me), :],
-            send_sem=back_send.at[peer],
-            recv_sem=back_recv.at[me],
-            device_id={"expert": peer},
-            device_id_type=MESH,
-        )
-
-    def came_back(peer):
-        return pltpu.make_async_remote_copy(
-            src_ref=rows.at[block(peer), :],
-            dst_ref=returned.at[block(peer), :],
-            send_sem=back_send.at[peer],
-            recv_sem=back_recv.at[peer],
-            device_id={"expert": peer},
-            device_id_type=MESH,
-        )
-
-    for k in range(1, devices):
-        back(lax.rem(me + k, devices)).start()
-    returned[block(me), :] = rows[block(me), :]
+    lax.fori_loop(0, 2 * count + 2 * SKEW * last, step, 0)
+    returned[block(me), :] = rows[:cap, :]
 
     def drain(c, carry):
         for s in (0, 1):
@@ -237,16 +237,28 @@
 
         return carry
 
-    lax.fori_loop(0, count, drain, 0)
-    for k in range(1, devices):
-        dispatch(lax.rem(me + k, devices)).wait_send()
-    for k in range(1, devices):
-        came_back(lax.rem(me + devices - k, devices)).wait_recv()
-    coarse = jnp.dot(high[...], returned[...], preferred_element_type=jnp.float32)
-    fine = jnp.dot(low[...], returned[...], preferred_element_type=jnp.float32)
+    lax.fori_loop(0, 2 * count, drain, 0)
+    for slot in range(1, devices):
+        dispatch(slot).wait_send()
+    for slot in range(1, devices):
+        peer = partner(slot)
+        pltpu.make_async_remote_copy(
+            src_ref=rows.at[slot * cap : (slot + 1) * cap, :],
+            dst_ref=returned.at[block(peer), :],
+            send_sem=back_send.at[slot],
+            recv_sem=back_recv.at[slot],
+            device_id={"expert": peer},
+            device_id_type=MESH,
+        ).wait_recv()
+    coarse = jnp.zeros(mixed.shape, jnp.float32)
+    fine = jnp.zeros(mixed.shape, jnp.float32)
+    for q in range(devices // held):
+        came = returned[q * held * cap : (q + 1) * held * cap, :]
+        coarse += jnp.dot(high[...], came, preferred_element_type=jnp.float32)
+        fine += jnp.dot(low[...], came, preferred_element_type=jnp.float32)
     mixed[...] = ((coarse * 256.0 + fine) * (1.0 / 65536.0)).astype(mixed.dtype)
-    for k in range(1, devices):
-        back(lax.rem(me + k, devices)).wait_send()
+    for slot in range(1, devices):
+        back(slot).wait_send()
 
 
 def along_line(outgoing, high, low, w_gate, w_up, w_down, devices, groups, cap):
@@ -254,9 +266,9 @@
     hidden_width = w_gate.shape[1]
     chunk = min(CHUNK, hidden_width)
     count = hidden_width // chunk
-    half = devices * cap // 2
+    part = devices * cap // 4
     in_vmem, in_place = pl.BlockSpec(memory_space=pltpu.VMEM), pl.BlockSpec(memory_space=pl.ANY)
-    flops = 2 * 3 * 2 * half * hidden_width * width_part
+    flops = 2 * 3 * 4 * part * hidden_width * width_part
     return pl.pallas_call(
         functools.partial(line_kernel, devices, groups, cap, chunk),
         out_shape=jax.ShapeDtypeStruct((token_count, width_part), jnp.bfloat16),
@@ -266,15 +278,15 @@
             pltpu.VMEM((hidden_width, width_part), jnp.bfloat16),
             pltpu.VMEM((hidden_width, width_part), jnp.bfloat16),
             pltpu.VMEM((hidden_width, width_part), jnp.bfloat16),
-            pltpu.VMEM((2 * half, width_part), jnp.bfloat16),
-            pltpu.VMEM((2, count, half, 2 * chunk), jnp.bfloat16),
-            pltpu.VMEM((half, 2 * chunk), jnp.float32),
-            pltpu.VMEM((2, count, half, chunk), jnp.bfloat16),
-            pltpu.VMEM((2, half, width_part), jnp.float32),
-            pltpu.VMEM((2 * half, width_part), jnp.bfloat16),
+            pltpu.VMEM((4 * part, width_part), jnp.bfloat16),
+            pltpu.VMEM((2, 2 * count, part, 2 * chunk), jnp.bfloat16),
+            pltpu.VMEM((part, 2 * chunk), jnp.float32),
+            pltpu.VMEM((2, 2 * count, part, chunk), jnp.bfloat16),
+            pltpu.VMEM((4, part, width_part), jnp.float32),
+            pltpu.VMEM((4 * part, width_part), jnp.bfloat16),
             *[pltpu.SemaphoreType.DMA((count,))] * 3,
             *[pltpu.SemaphoreType.DMA((devices,))] * 4,
-            *[pltpu.SemaphoreType.DMA((2, count))] * 4,
+            *[pltpu.SemaphoreType.DMA((2, 2 * count))] * 4,
         ],
         compiler_params=pltpu.CompilerParams(
             collective_id=0, has_side_effects=True, vmem_limit_bytes=60 * 2**20
@@ -282,7 +294,7 @@
         cost_estimate=pl.CostEstimate(
             flops=flops,
             bytes_accessed=3 * 2 * hidden_width * width_part,
-            transcendentals=half * hidden_width,
+            transcendentals=2 * part * hidden_width,
         ),
     )(outgoing, high, low, w_gate, w_up, w_down)
 
@@ -314,6 +326,7 @@
         partial_out.reshape(devices, cap, width_part), "expert", split_axis=0, concat_axis=0, tiled=True
     )
     selector = (high.astype(jnp.float32) * 256.0 + low.astype(jnp.float32)) / 65536.0
+    selector = jnp.tile(selector, (1, devices // EXPERTS))
     mixed = jnp.dot(
         selector, returned.reshape(total_rows, width_part), precision=lax.Precision.HIGHEST
     )
@@ -332,18 +345,19 @@
     position = jnp.dot(
         earlier, routed.astype(jnp.bfloat16), preferred_element_type=jnp.float32
     ).astype(jnp.int32)
-    slots = jnp.arange(cap, dtype=jnp.int32)
-    placed = (position[:, :, None] == slots) & routed[:, :, None]
-    outgoing = jnp.einsum(
-        "tec,td->ecd", placed.astype(jnp.bfloat16), tokens, preferred_element_type=jnp.float32
+    column = jnp.arange(EXPERTS * cap, dtype=jnp.int32)
+    target = jnp.where(routed, position + cap * jnp.arange(EXPERTS, dtype=jnp.int32), -1)
+
+    def spread(values):
+        chosen = [jnp.where(column == target[:, e : e + 1], values[:, e : e + 1], 0) for e in range(EXPERTS)]
+        return sum(chosen).astype(jnp.bfloat16)
+
+    outgoing = lax.dot_general(
+        spread(routed.astype(jnp.int32)), tokens, (((0,), (0,)), ((), ())), preferred_element_type=jnp.float32
     ).astype(jnp.bfloat16)
-
-    def selector(digit):
-        chosen = jnp.where(placed, digit[:, :, None], 0).astype(jnp.bfloat16)
-        return jnp.tile(chosen.reshape(token_count, EXPERTS * cap), (1, devices // EXPERTS))
-
-    high, low = selector(units // 256), selector(units % 256)
-    plan = along_line if groups <= LINE else by_collectives
+    outgoing = outgoing.reshape(EXPERTS, cap, tokens.shape[1])
+    high, low = spread(units // 256), spread(units % 256)
+    plan = along_line if groups <= LINE and devices in ORDER else by_collectives
     return plan(outgoing, high, low, w_gate, w_up, w_down, devices, groups, cap)
 
 

time: 161 us -> 148 us (0.919)
  Pallas kernels: 154 us -> 142 us
    pallas_call x1, Pallas kernels: 154 us -> 142 us  [along_line(): pl.pallas_call(functools.partial(line_kernel, devices, groups, cap, chunk...]
where the time goes in v2:
time: 148 us
  Pallas kernels  142 us (96%)
  other arithmetic  2.4 us (2%)
  local copies, waits for them, and re-layouts  1.82 us (1%)
    pallas_call x1, Pallas kernels, along_line(): pl.pallas_call(functools.partial(line_kernel, devices, groups, cap, chunk...  142 us

profile of v2, /device:TPU:1, one launch (start us, length us, event | category | flops | bytes accessed | tf_op | source)
XLA Modules:
  0.0 147.9 jit_solution(18312261241238835210)
XLA Ops:
  0.0 0.0 copy-start
  0.0 0.7 fusion.11
  0.8 0.1 fusion.1
  0.9 0.7 select_reduce_fusion
  1.7 0.9 add_convert_fusion
  2.6 0.0 copy-done
  2.6 1.3 convolution_convert_fusion
  3.9 142.2 %shard_map.64 = bf16[128,1536]{1,0:T(8,128)(2,1)} custom-call(bf16[4,48,1536]{2,1,0:T(8,128)(2,1)} %bitcast.35, bf16[128,192]{1,0:T(8,128)(2,1)} %get-tuple-element.6.high, bf16[128,192]{1,0:T(8,128)(2,1)} %get-tuple-element.5.low, bf16[1,4096,1536]{2,1,0:T(8,128)(2,1)} %w_gate.1, bf16[1,4096,1536]{2,1,0:T(8,128)(2,1)} %w_up.1, bf16[1,4096,1536]{2,1,0:T(8,128)(2,1)} %w_down.1), custom_call_target="tpu_custom_call" | custom-call | flops 14495514624 | bytes 37748736 | tf_op jit(solution)/shard_map/pallas_call | solution.py:272
  146.1 1.8 %copy.10 = bf16[128,1536]{1,0:T(8,128)(2,1)} copy(bf16[128,1536]{1,0:T(8,128)(2,1)} %shard_map.64) | data formatting | bytes 786432
  (5 shorter events, 0.1 us)
Async XLA Ops:
  0.0 2.6 %copy-start = (bf16[128,1536]{1,0:T(8,128)(2,1)S(1)}, bf16[128,1536]{1,0:T(8,128)(2,1)}, u32[]{:S(2)}) copy-start(bf16[128,1536]{1,0:T(8,128)(2,1)} %param.6) | copy-start | bytes 1179652
